TPU v7x, 256 devices: a whole 4x4x8 slice. The times are simulated.
256 devices in a mesh: wide: 32 (over y, z), narrow: 8 (over x, core).
Axes of the slice: x: 4, y: 4, z: 8, core: 2. Of those that a mesh axis runs over, the one named last changes fastest.
Arguments:
- residual: bfloat16 [32, 8, 2048, 256], P('wide', 'narrow'), may hold values from -6 to 6
- scaling: float32 [32, 8, 2048], P('wide', 'narrow'), may hold values from 0.25 to 1
- local_inverse: bfloat16 [32, 8, 2048, 2048], P('wide', 'narrow'), may hold values from -0.125 to 0.125
- coarse_basis: bfloat16 [32, 8, 24, 2048], P('wide', 'narrow'), may hold values from -0.125 to 0.125
- primal_map: int32 [32, 8, 24], P('wide', 'narrow'), may hold values from 0 to 191
- slot_index: int32 [32, 8, 10, 256], P('wide', 'narrow'), may hold values from 0 to 2047, as said below
- slot_length: int32 [32, 8, 10], P('wide', 'narrow'), may hold values from 0 to 256, as said below
- coarse_sub: float32 [32, 192, 192], P('wide'), may hold values from -0.4375 to 0.4375
- coarse_pivot: float32 [32, 192, 192], P('wide'), as said below
Outputs:
- interface_sum: float32 [32, 8, 2048, 256], P('wide', 'narrow')
Inputs may be any that keep to these rules, and one draw needn't show every extreme that they name: `slot_index`: within one slot of one subdomain the 256 entries are distinct. `slot_length`: paired slots have equal lengths: slot j of subdomain (w, n) and slot n of (w, j); slot 8 of (w, n) and slot 9 of (w - 1, n). A subdomain's own narrow slot n, the slot 8 of slab 0 and the slot 9 of slab 32 - 1 have length 0. `coarse_pivot`: Symmetric.
All inputs are finite; a program needn't handle non-finite values.
Results may differ from a plain program's by a relative error of at most 0.0039.
The roundings to bfloat16 on the way count: a program that leaves them out, or rounds other values in their place, can miss the bound.
Values may be sent and summed in bfloat16 or wider, within the bound.
A program may use at most 128 MiB of HBM per device.

v0:
```python
import jax
import jax.numpy as jnp
from jax import lax
from jax.sharding import PartitionSpec as P

highest = lax.Precision.HIGHEST


def entering(part, axis, combine, identity, reverse):
    count = lax.axis_size(axis)
    place = lax.axis_index(axis)
    ahead = count - 1 - place if reverse else place
    gathered = jax.tree.map(lambda a: lax.all_gather(a, axis), part)
    state = jax.tree.map(lambda a, e: jnp.zeros_like(a) + jnp.asarray(e, a.dtype), part, identity)

    def one(turn, state):
        source = count - 1 - turn if reverse else turn
        return combine(
            state, jax.tree.map(lambda a: lax.dynamic_index_in_dim(a, source, 0, False), gathered)
        )

    return lax.fori_loop(0, ahead, one, state)


def shifted(block, axis, distance):
    devices = range(lax.axis_size(axis))
    route = [(i - distance, i) for i in devices if i - distance in devices]
    return lax.ppermute(block, axis, route)


def exact_dot(left, right):
    return jnp.dot(left, right, precision=highest, preferred_element_type=jnp.float32)


def compose(earlier, later):
    return (exact_dot(later[0], earlier[0]), exact_dot(later[0], earlier[1]) + later[1])


def coarse_solve(coarse_rhs, sub_block, pivot_block):
    order = sub_block.shape[0]
    identity = jnp.eye(order, dtype=jnp.float32)
    empty = jnp.zeros_like(coarse_rhs)
    sub_trans = sub_block.T
    before = entering((-sub_block, coarse_rhs), "wide", compose, (identity, empty), False)
    chain_y = coarse_rhs - exact_dot(sub_block, before[1])
    pivoted = exact_dot(pivot_block, chain_y)
    after = entering(
        (-sub_trans, exact_dot(sub_trans, pivoted)), "wide", compose, (identity, empty), True
    )
    return pivoted - after[1]


def body(
    residual,
    scaling,
    local_inverse,
    coarse_basis,
    primal_map,
    slot_index,
    slot_length,
    coarse_sub,
    coarse_pivot,
):
    groups = lax.axis_size("narrow")
    weights = scaling[0, 0]
    weighted = (weights[:, None] * residual[0, 0].astype(jnp.float32)).astype(jnp.bfloat16)
    local_part = jnp.dot(local_inverse[0, 0], weighted, preferred_element_type=jnp.float32)
    basis = coarse_basis[0, 0]
    primal = jnp.dot(basis, weighted, preferred_element_type=jnp.float32)
    order = coarse_sub.shape[1]
    one_hot = (primal_map[0, 0][:, None] == jnp.arange(order, dtype=jnp.int32)[None, :]).astype(
        jnp.float32
    )
    assembly = lax.dot_general(
        one_hot,
        primal,
        (((0,), (0,)), ((), ())),
        precision=highest,
        preferred_element_type=jnp.float32,
    )
    coarse_rhs = lax.psum(assembly, "narrow")
    coarse_sol = coarse_solve(coarse_rhs, coarse_sub[0], coarse_pivot[0])
    coarse_vals = exact_dot(one_hot, coarse_sol)
    spread = lax.dot_general(
        basis.astype(jnp.float32),
        coarse_vals,
        (((0,), (0,)), ((), ())),
        precision=highest,
        preferred_element_type=jnp.float32,
    )
    combined = (weights[:, None] * (local_part + spread)).astype(jnp.bfloat16)
    indices = slot_index[0, 0]
    lengths = slot_length[0, 0]
    capacity = indices.shape[1]
    live_mask = jnp.arange(capacity, dtype=jnp.int32)[None, :] < lengths[:, None]
    outgoing = jnp.where(live_mask[:, :, None], combined[indices], jnp.zeros((), jnp.bfloat16))
    narrow_in = lax.all_to_all(outgoing[:groups], "narrow", split_axis=0, concat_axis=0, tiled=True)
    below = shifted(outgoing[groups + 1], "wide", 1)
    above = shifted(outgoing[groups], "wide", -1)
    incoming = jnp.concatenate([narrow_in, below[None], above[None]], axis=0)
    columns = combined.shape[1]
    summed = (
        combined.astype(jnp.float32)
        .at[indices.reshape(-1)]
        .add(incoming.reshape(-1, columns).astype(jnp.float32))
    )
    return summed[None, None]


def solution(mesh):
    in_specs = (
        P("wide", "narrow", None, None),
        P("wide", "narrow", None),
        P("wide", "narrow", None, None),
        P("wide", "narrow", None, None),
        P("wide", "narrow", None),
        P("wide", "narrow", None, None),
        P("wide", "narrow", None),
        P("wide", None, None),
        P("wide", None, None),
    )
    out_specs = P("wide", "narrow", None, None)
    return jax.shard_map(body, mesh=mesh, in_specs=in_specs, out_specs=out_specs, check_vma=False)
```

profile of v0, /device:TPU:1, one launch (start us, length us, event | category | flops | bytes accessed | tf_op | source)
XLA Modules:
  0.0 475.1 jit_solution(10385188580187387895)
XLA Ops:
  7.4 2.1 fusion.15
  9.5 1.7 fusion.27
  12.0 66.6 %all-reduce.2.cloned.1.call-done = f32[192,256]{1,0:T(8,128)} async-done(((f32[192,256]{1,0:T(8,128)}), f32[192,256]{1,0:T(8,128)}) %all-reduce.2.cloned.1.call-update) | async-done | bytes 196624 | tf_op jit(solution)/shard_map/psum | solution.py:81
  79.6 26.3 %all-gather.8.cloned.1.call-done = f32[32,192,192]{2,1,0:T(8,128)} async-done(((f32[1,192,192]{2,1,0:T(8,128)}), f32[32,192,192]{2,1,0:T(8,128)}) %all-gather.8.cloned.1.call-update) | async-done | bytes 4718608 | tf_op jit(solution)/shard_map/all_gather | solution.py:13
  105.9 88.2 %all-gather.10.cloned.1.call-done = f32[6144,256]{1,0:T(8,128)} async-done(((f32[192,256]{1,0:T(8,128)}), f32[6144,256]{1,0:T(8,128)}) %all-gather.10.cloned.1.call-update) | async-done | bytes 6291472 | tf_op jit(solution)/shard_map/all_gather | solution.py:13
  197.3 6.5 %fusion.6 = f32[256,2048]{1,0:T(8,128)S(1)} fusion(bf16[1,1,2048,2048]{3,2,1,0:T(8,128)(2,1)} %param.15, bf16[1,1,2048,256]{3,2,1,0:T(8,128)(2,1)} %param.13, f32[2048]{0:T(1024)S(1)} %bitcast.96), kind=kOutput, calls=%fused_computation.10 | convolution fusion | flops 2149056512 | bytes 11542528 | tf_op jit(solution)/shard_map/dot_general | solution.py:67
  203.7 78.7 %all-gather.12.cloned.1.call-done = f32[6144,192]{1,0:T(8,128)} async-done(((f32[192,192]{1,0:T(8,128)}), f32[6144,192]{1,0:T(8,128)}) %all-gather.12.cloned.1.call-update) | async-done | bytes 4718608 | tf_op jit(solution)/shard_map/all_gather | solution.py:13
  282.5 88.4 %all-gather.14.cloned.1.call-done = f32[6144,256]{1,0:T(8,128)} async-done(((f32[192,256]{1,0:T(8,128)}), f32[6144,256]{1,0:T(8,128)}) %all-gather.14.cloned.1.call-update) | async-done | bytes 6291472 | tf_op jit(solution)/shard_map/all_gather | solution.py:13
  370.9 43.4 %while.27 = (s32[]{:T(128)}, f32[192,256]{1,0:T(8,128)S(1)}, s32[]{:T(128)}, f32[32,192,192]{2,1,0:T(8,128)}, f32[32,192,256]{2,1,0:T(8,128)}, /*index=5*/s32[]{:T(128)}, s32[]{:T(128)}, s32[]{:T(128)}, s32[]{:T(128)}) while((s32[]{:T(128)}, f32[192,256]{1,0:T(8,128)S(1)}, s32[]{:T(128)}, f32[32,192,192]{2,1,0:T(8,128)}, ...), condition=%wide.region_4.5_spmd, body=%wide.region_3.4_spmd.sunk | while | flops 113295368 | bytes 1180811 | solution.py:22
  371.0 1.3 convolution_add_fusion.6
  375.2 1.3 convolution_add_fusion.6
  376.6 1.3 convolution_add_fusion.6
  378.0 1.3 convolution_add_fusion.6
  379.4 1.3 convolution_add_fusion.6
  380.8 1.3 convolution_add_fusion.6
  382.2 1.3 convolution_add_fusion.6
  383.6 1.3 convolution_add_fusion.6
  385.0 1.3 convolution_add_fusion.6
  386.4 1.3 convolution_add_fusion.6
  387.8 1.3 convolution_add_fusion.6
  389.2 1.3 convolution_add_fusion.6
  390.6 1.3 convolution_add_fusion.6
  392.0 1.3 convolution_add_fusion.6
  393.4 1.3 convolution_add_fusion.6
  394.8 1.3 convolution_add_fusion.6
  396.2 1.3 convolution_add_fusion.6
  397.6 1.3 convolution_add_fusion.6
  399.0 1.3 convolution_add_fusion.6
  400.4 1.3 convolution_add_fusion.6
  401.8 1.3 convolution_add_fusion.6
  403.2 1.3 convolution_add_fusion.6
  404.6 1.3 convolution_add_fusion.6
  406.0 1.3 convolution_add_fusion.6
  407.4 1.3 convolution_add_fusion.6
  408.8 1.3 convolution_add_fusion.6
  410.2 1.3 convolution_add_fusion.6
  411.6 1.3 convolution_add_fusion.6
  413.0 1.3 convolution_add_fusion.6
  414.6 2.0 fusion.12
  417.1 8.1 %gather_fusion = bf16[2560,256]{1,0:T(8,128)(2,1)} fusion(bf16[2048,256]{1,0:T(8,128)(2,1)S(1)} %copy.14, s32[3072]{0:T(1024)S(1)} %pad_clamp_fusion), kind=kCustom, calls=%fused_computation | custom fusion | bytes 2631680 | tf_op jit(solution)/shard_map/gather | solution.py:96
  425.3 1.6 broadcast_select_fusion
  428.0 5.6 %all-to-all-start = ((bf16[8,256,256]{2,1,0:T(8,128)(2,1)}), bf16[8,256,256]{2,1,0:T(8,128)(2,1)}, u32[]{:S(2)}, u32[]{:S(2)}) async-start(bf16[8,256,256]{2,1,0:T(8,128)(2,1)} %slice.14), calls=%async_computation | async-start | bytes 2097152 | tf_op jit(solution)/shard_map/all_to_all | solution.py:97
  433.7 1.7 collective-permute-start
  436.8 1.6 copy.15
  438.4 3.8 collective-permute-done.1
  442.2 6.7 %all-to-all-done = bf16[8,256,256]{2,1,0:T(8,128)(2,1)} async-done(((bf16[8,256,256]{2,1,0:T(8,128)(2,1)}), bf16[8,256,256]{2,1,0:T(8,128)(2,1)}, u32[]{:S(2)}, u32[]{:S(2)}) %all-to-all-start) | async-done | bytes 1048608 | tf_op jit(solution)/shard_map/all_to_all | solution.py:97
  448.8 1.4 pad_maximum_fusion
  450.2 17.2 %scatter_custom_fusion = f32[2048,256]{1,0:T(8,128)} fusion(f32[2048,256]{1,0:T(8,128)} %copy.15, s32[2560]{0:T(1024)S(1)} %fusion.32, bf16[2560,256]{1,0:T(8,128)(2,1)S(1)} %bitcast.86), kind=kCustom, calls=%fused_computation.14 | custom fusion | flops 1310720 | bytes 3407872 | tf_op jit(solution)/shard_map/scatter-add | solution.py:105
  (79 shorter events, 11.0 us)
Async XLA Ops:
  7.4 188.1 %copy-start = (f32[1,192,192]{2,1,0:T(8,128)S(1)}, f32[1,192,192]{2,1,0:T(8,128)}, u32[]{:S(2)}) copy-start(f32[1,192,192]{2,1,0:T(8,128)} %param.21) | copy-start | bytes 442372
  7.4 3.9 copy-start.1
  7.4 71.3 %all-reduce.2.cloned.1.call-start = ((), (), s32[]{:S(2)}) async-start(), calls=%async_computation.1 | async-start | bytes 393216 | tf_op jit(solution)/shard_map/psum | solution.py:81
  11.2 94.7 %all-gather.8.cloned.1.call-start = ((), (), s32[]{:S(2)}) async-start(), calls=%async_computation.2 | async-start | bytes 6488064 | tf_op jit(solution)/shard_map/all_gather | solution.py:13
  12.0 182.2 %all-gather.10.cloned.1.call-start = ((), (), s32[]{:S(2)}) async-start(), calls=%async_computation.3 | async-start | bytes 6488064 | tf_op jit(solution)/shard_map/all_gather | solution.py:13
  78.7 203.8 %all-gather.12.cloned.1.call-start = ((), (), s32[]{:S(2)}) async-start(), calls=%async_computation.4 | async-start | bytes 6488064 | tf_op jit(solution)/shard_map/all_gather | solution.py:13
  79.6 291.3 %all-gather.14.cloned.1.call-start = ((), (), s32[]{:S(2)}) async-start(), calls=%async_computation.5 | async-start | bytes 6488064 | tf_op jit(solution)/shard_map/all_gather | solution.py:13
  194.2 0.9 copy-start.2
  194.2 2.9 copy-start.3
  194.2 2.9 copy-start.7
  194.2 3.0 copy-start.5
  370.9 43.4 %copy-start.6 = (s32[1,1,24]{2,1,0:T(1,128)S(1)}, s32[1,1,24]{2,1,0:T(1,128)}, u32[]{:S(2)}) copy-start(s32[1,1,24]{2,1,0:T(1,128)} %param.17) | copy-start | bytes 292
  426.9 9.8 %copy-start.4 = (s32[1,1,10,256]{3,1,2,0:T(1,128)S(1)}, s32[1,1,10,256]{3,1,2,0:T(1,128)}, u32[]{:S(2)}) copy-start(s32[1,1,10,256]{3,1,2,0:T(1,128)} %param.18) | copy-start | bytes 30724
  428.0 20.8 %all-to-all-start = ((bf16[8,256,256]{2,1,0:T(8,128)(2,1)}), bf16[8,256,256]{2,1,0:T(8,128)(2,1)}, u32[]{:S(2)}, u32[]{:S(2)}) async-start(bf16[8,256,256]{2,1,0:T(8,128)(2,1)} %slice.14), calls=%async_computation | async-start | bytes 2097152 | tf_op jit(solution)/shard_map/all_to_all | solution.py:97
  433.7 4.7 collective-permute-start
  435.4 6.8 %collective-permute-start.1 = (bf16[256,256]{1,0:T(8,128)(2,1)S(1)}, bf16[256,256]{1,0:T(8,128)(2,1)S(1)}, u32[]{:S(2)}, u32[]{:S(2)}) collective-permute-start(bf16[256,256]{1,0:T(8,128)(2,1)S(1)} %get-tuple-element.156), channel_id=1, source_target_pairs={{8,0},{16,8},{24,16},{32,24},{40,32},{48,40},{56,48},{64,56},{72,6... | collective-permute-start | bytes 393224 | tf_op jit(solution)/shard_map/ppermute | solution.py:28
Sparse Core Ops, SparseCore 0:
  11.3 67.2 all-reduce.1
Sparse Core Ops, SparseCore 1:
  14.3 91.6 all-gather.7
  108.7 85.4 all-gather.9
  197.0 85.5 all-gather.11
  285.4 85.4 all-gather.13
where the time goes:
time: 476 us; the launch traced here: 475 us
  waiting for transfers between devices  359 us (75%)
  matrix products  56.1 us (12%)
  other arithmetic  21.8 us (5%)
  between operations  15.3 us (3%)
  local copies, waits for them, and re-layouts  12.9 us (3%)
  starting transfers between devices  8.84 us (2%)
    all_gather x4, waiting for transfers between devices, entering(): gathered = jax.tree.map(lambda a: lax.all_gather(a, axis), part)  282 us
    psum x1, waiting for transfers between devices, body(): coarse_rhs = lax.psum(assembly, 'narrow')  66.6 us
    dot_general x35, matrix products, exact_dot(): jnp.dot(left, right, precision=highest, preferred_element_type=jnp.float32)  43.8 us
    scatter-add x1, other arithmetic, body(): summed = combined.astype(jnp.float32).at[indices.reshape(-1)].add(incomin...  17.2 us
  transfers between devices with their start and end apart: 8, of which 7 were waited for; matrix products, arithmetic and copies ran while one was open for 2% of the time, Pallas kernels for 0%

commit v1 on v0

--- a/solution.py
+++ b/solution.py
@@ -78,7 +78,7 @@
         precision=highest,
         preferred_element_type=jnp.float32,
     )
-    coarse_rhs = lax.psum(assembly, "narrow")
+    coarse_rhs = jnp.sum(lax.all_gather(assembly, "narrow"), axis=0)
     coarse_sol = coarse_solve(coarse_rhs, coarse_sub[0], coarse_pivot[0])
     coarse_vals = exact_dot(one_hot, coarse_sol)
     spread = lax.dot_general(

time: 476 us -> 500 us (1.050)
  waiting for transfers between devices: 359 us -> 384 us
    psum x1 -> x0, waiting for transfers between devices: 66.6 us -> none  [body(): coarse_rhs = lax.psum(assembly, 'narrow')]
    all_gather x4, waiting for transfers between devices: 282 us -> 343 us  [entering(): gathered = jax.tree.map(lambda a: lax.all_gather(a, axis), part)]
    all_gather x0 -> x1, waiting for transfers between devices: none -> 30.4 us  [body(): coarse_rhs = jnp.sum(lax.all_gather(assembly, 'narrow'), axis=0)]
  transfers between devices with their start and end apart: 8 -> 8, of which waited for: 7 -> 7; matrix products, arithmetic and copies ran while one was open for 2% -> 3% of each run, Pallas kernels for 0% -> 0%
where the time goes in v1:
time: 500 us; the launch traced here: 499 us
  waiting for transfers between devices  384 us (77%)
  matrix products  55.2 us (11%)
  other arithmetic  24 us (5%)
  between operations  13.4 us (3%)
  local copies, waits for them, and re-layouts  12.9 us (3%)
  starting transfers between devices  8.11 us (2%)
    all_gather x4, waiting for transfers between devices, entering(): gathered = jax.tree.map(lambda a: lax.all_gather(a, axis), part)  343 us
    dot_general x35, matrix products, exact_dot(): jnp.dot(left, right, precision=highest, preferred_element_type=jnp.float32)  43.8 us
    all_gather x1, waiting for transfers between devices, body(): coarse_rhs = jnp.sum(lax.all_gather(assembly, 'narrow'), axis=0)  30.4 us
    scatter-add x1, other arithmetic, body(): summed = combined.astype(jnp.float32).at[indices.reshape(-1)].add(incomin...  17.2 us
  transfers between devices with their start and end apart: 8, of which 7 were waited for; matrix products, arithmetic and copies ran while one was open for 3% of the time, Pallas kernels for 0%

profile of v1, /device:TPU:1, one launch (start us, length us, event | category | flops | bytes accessed | tf_op | source)
XLA Modules:
  0.0 499.0 jit_solution(1637106620475140258)
XLA Ops:
  6.5 2.1 fusion.15
  8.7 1.7 fusion.27
  11.2 30.4 %all-gather.12.cloned.1.call-done = f32[1536,256]{1,0:T(8,128)} async-done(((f32[192,256]{1,0:T(8,128)}), f32[1536,256]{1,0:T(8,128)}) %all-gather.12.cloned.1.call-update) | async-done | bytes 1572880 | tf_op jit(solution)/shard_map/all_gather | solution.py:81
  41.6 2.2 reduce_sum.9
  44.8 87.8 %all-gather.10.cloned.1.call-done = f32[32,192,192]{2,1,0:T(8,128)} async-done(((f32[1,192,192]{2,1,0:T(8,128)}), f32[32,192,192]{2,1,0:T(8,128)}) %all-gather.10.cloned.1.call-update) | async-done | bytes 4718608 | tf_op jit(solution)/shard_map/all_gather | solution.py:13
  132.6 88.3 %all-gather.14.cloned.1.call-done = f32[6144,256]{1,0:T(8,128)} async-done(((f32[192,256]{1,0:T(8,128)}), f32[6144,256]{1,0:T(8,128)}) %all-gather.14.cloned.1.call-update) | async-done | bytes 6291472 | tf_op jit(solution)/shard_map/all_gather | solution.py:13
  223.9 6.5 %fusion.6 = f32[256,2048]{1,0:T(8,128)S(1)} fusion(bf16[1,1,2048,2048]{3,2,1,0:T(8,128)(2,1)} %param.15, bf16[1,1,2048,256]{3,2,1,0:T(8,128)(2,1)} %param.13, f32[2048]{0:T(1024)S(1)} %bitcast.97), kind=kOutput, calls=%fused_computation.10 | convolution fusion | flops 2149056512 | bytes 11542528 | tf_op jit(solution)/shard_map/dot_general | solution.py:67
  230.4 78.6 %all-gather.16.cloned.1.call-done = f32[6144,192]{1,0:T(8,128)} async-done(((f32[192,192]{1,0:T(8,128)}), f32[6144,192]{1,0:T(8,128)}) %all-gather.16.cloned.1.call-update) | async-done | bytes 4718608 | tf_op jit(solution)/shard_map/all_gather | solution.py:13
  309.0 88.2 %all-gather.18.cloned.1.call-done = f32[6144,256]{1,0:T(8,128)} async-done(((f32[192,256]{1,0:T(8,128)}), f32[6144,256]{1,0:T(8,128)}) %all-gather.18.cloned.1.call-update) | async-done | bytes 6291472 | tf_op jit(solution)/shard_map/all_gather | solution.py:13
  397.2 43.4 %while.27 = (s32[]{:T(128)}, f32[192,256]{1,0:T(8,128)S(1)}, s32[]{:T(128)}, f32[32,192,192]{2,1,0:T(8,128)}, f32[32,192,256]{2,1,0:T(8,128)}, /*index=5*/s32[]{:T(128)}, s32[]{:T(128)}, s32[]{:T(128)}, s32[]{:T(128)}) while((s32[]{:T(128)}, f32[192,256]{1,0:T(8,128)S(1)}, s32[]{:T(128)}, f32[32,192,192]{2,1,0:T(8,128)}, ...), condition=%wide.region_4.5_spmd, body=%wide.region_3.4_spmd.sunk | while | flops 113295368 | bytes 1180811 | solution.py:22
  397.2 1.3 convolution_add_fusion.6
  398.6 1.3 convolution_add_fusion.6
  400.0 1.3 convolution_add_fusion.6
  401.4 1.3 convolution_add_fusion.6
  402.8 1.3 convolution_add_fusion.6
  404.2 1.3 convolution_add_fusion.6
  405.6 1.3 convolution_add_fusion.6
  407.0 1.3 convolution_add_fusion.6
  408.4 1.3 convolution_add_fusion.6
  409.8 1.3 convolution_add_fusion.6
  411.2 1.3 convolution_add_fusion.6
  412.6 1.3 convolution_add_fusion.6
  414.0 1.3 convolution_add_fusion.6
  415.4 1.3 convolution_add_fusion.6
  416.8 1.3 convolution_add_fusion.6
  418.2 1.3 convolution_add_fusion.6
  419.6 1.3 convolution_add_fusion.6
  421.0 1.3 convolution_add_fusion.6
  422.4 1.3 convolution_add_fusion.6
  425.2 1.3 convolution_add_fusion.6
  426.6 1.3 convolution_add_fusion.6
  429.4 1.3 convolution_add_fusion.6
  430.8 1.3 convolution_add_fusion.6
  432.2 1.3 convolution_add_fusion.6
  433.6 1.3 convolution_add_fusion.6
  435.0 1.3 convolution_add_fusion.6
  436.4 1.3 convolution_add_fusion.6
  437.8 1.3 convolution_add_fusion.6
  439.2 1.3 convolution_add_fusion.6
  442.5 8.1 %gather_fusion = bf16[2560,256]{1,0:T(8,128)(2,1)} fusion(bf16[2048,256]{1,0:T(8,128)(2,1)S(1)} %copy.14, s32[3072]{0:T(1024)S(1)} %pad_clamp_fusion), kind=kCustom, calls=%fused_computation | custom fusion | bytes 2631680 | tf_op jit(solution)/shard_map/gather | solution.py:96
  450.6 1.6 broadcast_select_fusion
  453.3 5.3 %all-to-all-start = ((bf16[8,256,256]{2,1,0:T(8,128)(2,1)}), bf16[8,256,256]{2,1,0:T(8,128)(2,1)}, u32[]{:S(2)}, u32[]{:S(2)}) async-start(bf16[8,256,256]{2,1,0:T(8,128)(2,1)} %slice.14), calls=%async_computation | async-start | bytes 2097152 | tf_op jit(solution)/shard_map/all_to_all | solution.py:97
  458.7 1.4 collective-permute-start
  461.4 1.6 copy.15
  463.0 3.8 collective-permute-done.1
  466.8 7.0 %all-to-all-done = bf16[8,256,256]{2,1,0:T(8,128)(2,1)} async-done(((bf16[8,256,256]{2,1,0:T(8,128)(2,1)}), bf16[8,256,256]{2,1,0:T(8,128)(2,1)}, u32[]{:S(2)}, u32[]{:S(2)}) %all-to-all-start) | async-done | bytes 1048608 | tf_op jit(solution)/shard_map/all_to_all | solution.py:97
  473.8 1.4 pad_maximum_fusion
  475.2 17.2 %scatter_custom_fusion = f32[2048,256]{1,0:T(8,128)} fusion(f32[2048,256]{1,0:T(8,128)} %copy.15, s32[2560]{0:T(1024)S(1)} %fusion.32, bf16[2560,256]{1,0:T(8,128)(2,1)S(1)} %bitcast.87), kind=kCustom, calls=%fused_computation.14 | custom fusion | flops 1310720 | bytes 3407872 | tf_op jit(solution)/shard_map/scatter-add | solution.py:105
  (80 shorter events, 12.1 us)
Async XLA Ops:
  6.5 215.6 %copy-start = (f32[1,192,192]{2,1,0:T(8,128)S(1)}, f32[1,192,192]{2,1,0:T(8,128)}, u32[]{:S(2)}) copy-start(f32[1,192,192]{2,1,0:T(8,128)} %param.21) | copy-start | bytes 442372
  6.5 3.9 copy-start.1
  6.5 35.1 %all-gather.12.cloned.1.call-start = ((), (), s32[]{:S(2)}) async-start(), calls=%async_computation.2 | async-start | bytes 1769472 | tf_op jit(solution)/shard_map/all_gather | solution.py:81
  10.4 122.2 %all-gather.10.cloned.1.call-start = ((), (), s32[]{:S(2)}) async-start(), calls=%async_computation.1 | async-start | bytes 6488064 | tf_op jit(solution)/shard_map/all_gather | solution.py:13
  11.1 209.7 %all-gather.14.cloned.1.call-start = ((), (), s32[]{:S(2)}) async-start(), calls=%async_computation.3 | async-start | bytes 6488064 | tf_op jit(solution)/shard_map/all_gather | solution.py:13
  43.8 265.1 %all-gather.16.cloned.1.call-start = ((), (), s32[]{:S(2)}) async-start(), calls=%async_computation.4 | async-start | bytes 6488064 | tf_op jit(solution)/shard_map/all_gather | solution.py:13
  44.7 352.4 %all-gather.18.cloned.1.call-start = ((), (), s32[]{:S(2)}) async-start(), calls=%async_computation.5 | async-start | bytes 6488064 | tf_op jit(solution)/shard_map/all_gather | solution.py:13
  220.9 0.9 copy-start.2
  220.9 2.9 copy-start.4
  220.9 2.9 copy-start.7
  220.9 3.0 copy-start.5
  397.1 43.5 %copy-start.6 = (s32[1,1,24]{2,1,0:T(1,128)S(1)}, s32[1,1,24]{2,1,0:T(1,128)}, u32[]{:S(2)}) copy-start(s32[1,1,24]{2,1,0:T(1,128)} %param.17) | copy-start | bytes 292
  397.2 43.7 %copy-start.3 = (bf16[1,1,24,2048]{3,2,1,0:T(8,128)(2,1)S(1)}, bf16[1,1,24,2048]{3,2,1,0:T(8,128)(2,1)}, u32[]{:S(2)}) copy-start(bf16[1,1,24,2048]{3,2,1,0:T(8,128)(2,1)} %param.16) | copy-start | bytes 294916
  453.3 20.5 %all-to-all-start = ((bf16[8,256,256]{2,1,0:T(8,128)(2,1)}), bf16[8,256,256]{2,1,0:T(8,128)(2,1)}, u32[]{:S(2)}, u32[]{:S(2)}) async-start(bf16[8,256,256]{2,1,0:T(8,128)(2,1)} %slice.14), calls=%async_computation | async-start | bytes 2097152 | tf_op jit(solution)/shard_map/all_to_all | solution.py:97
  458.7 4.3 collective-permute-start
  460.0 6.8 %collective-permute-start.1 = (bf16[256,256]{1,0:T(8,128)(2,1)S(1)}, bf16[256,256]{1,0:T(8,128)(2,1)S(1)}, u32[]{:S(2)}, u32[]{:S(2)}) collective-permute-start(bf16[256,256]{1,0:T(8,128)(2,1)S(1)} %get-tuple-element.156), channel_id=1, source_target_pairs={{8,0},{16,8},{24,16},{32,24},{40,32},{48,40},{56,48},{64,56},{72,6... | collective-permute-start | bytes 393224 | tf_op jit(solution)/shard_map/ppermute | solution.py:28
Sparse Core Ops, SparseCore 0:
  10.5 31.0 all-gather.11
  44.2 88.3 all-gather.9
  135.2 85.6 all-gather.13
  223.3 85.6 all-gather.15
  311.4 85.6 all-gather.17
